TPU v7x, 32 devices: a whole 2x2x4 slice. The times are simulated.
32 devices in a mesh: blk: 8 (over z, y), row: 4 (over x, core).
Axes of the slice: x: 2, y: 2, z: 4, core: 2. Of those that a mesh axis runs over, the one named last changes fastest.
Arguments:
- pool_embeds: bfloat16 [8192, 768], P('blk'), may hold values from -24 to 24
- target_samples: bfloat16 [2048, 768], P(('blk', 'row')), may hold values from -6 to 6
- reference_samples: bfloat16 [2048, 768], P(('blk', 'row')), may hold values from -6 to 6
Outputs:
- log_ratio: float32 [8192], P('blk')
- standardized: float32 [8192], P('blk')
All inputs are finite; a program needn't handle non-finite values.
Results may differ from a plain program's by a relative error of at most 0.0003.
Values may be sent and summed in bfloat16 or wider, within the bound.
A program may use at most 128 MiB of HBM per device.

v0:
```python
import jax
import jax.numpy as jnp
from jax import lax
from jax.sharding import PartitionSpec as P

KERNEL_GAIN = 30.0


def make_fold(pool_rows):
    pool_norms = jnp.sum(jnp.square(pool_rows.astype(jnp.float32)), axis=1)
    factor = KERNEL_GAIN / pool_rows.shape[1]

    def fold(running, pieces, offset):
        width = pieces[0].shape[0]
        joined = jnp.concatenate([pieces[0], pieces[1]], axis=0)
        joined_norms = jnp.sum(jnp.square(joined.astype(jnp.float32)), axis=1)
        products = jnp.dot(pool_rows, joined.T, preferred_element_type=jnp.float32)
        scores_all = (2.0 * products - pool_norms[:, None] - joined_norms[None, :]) * factor
        result = []
        for member in range(2):
            highest = running[2 * member]
            total = running[2 * member + 1]
            scores = scores_all[:, member * width : (member + 1) * width]
            new_high = jnp.maximum(highest, jnp.max(scores, axis=1))
            new_total = jnp.sum(jnp.exp(scores - new_high[:, None]), axis=1)
            result.append(new_high)
            result.append(new_total)
        return tuple(result)

    return fold


def start_state(count):
    lowest = jnp.full((count,), -1e30, jnp.float32)
    nothing = jnp.zeros((count,), jnp.float32)
    return (lowest, nothing, lowest, nothing)


def body(pool_embeds, target_samples, reference_samples):
    pool_count = pool_embeds.shape[0]
    fold = make_fold(pool_embeds)
    state = fold(
        start_state(pool_count),
        (
            lax.all_gather(target_samples, "blk", axis=0, tiled=True),
            lax.all_gather(reference_samples, "blk", axis=0, tiled=True),
        ),
        jnp.int32(0),
    )
    high_target, high_ref = lax.pmax((state[0], state[2]), "row")
    total_target, total_ref = lax.psum(
        (state[1] * jnp.exp(state[0] - high_target), state[3] * jnp.exp(state[2] - high_ref)), "row"
    )
    log_ratio = high_target + jnp.log(total_target) - (high_ref + jnp.log(total_ref))
    whole_count = pool_count * lax.axis_size("blk")
    first_sum, second_sum = lax.psum((jnp.sum(log_ratio), jnp.sum(jnp.square(log_ratio))), "blk")
    mean_value = first_sum / whole_count
    variance = second_sum / whole_count - jnp.square(mean_value)
    standardized = (log_ratio - mean_value) / jnp.sqrt(variance + 1e-05)
    return (log_ratio, standardized)


def solution(mesh):
    in_specs = (P("blk", None), P(("blk", "row"), None), P(("blk", "row"), None))
    out_specs = (P("blk"), P("blk"))
    return jax.shard_map(body, mesh=mesh, in_specs=in_specs, out_specs=out_specs, check_vma=False)
```

profile of v0, /device:TPU:0, one launch (start us, length us, event | category | flops | bytes accessed | tf_op | source)
XLA Modules:
  0.0 110.2 jit_solution(13617800607621359983)
XLA Ops:
  0.6 0.0 copy-start.1
  0.6 1.8 %multiply_reduce_fusion.1 = f32[1024]{0:T(1024)S(1)} fusion(bf16[1024,768]{1,0:T(8,128)(2,1)} %param.3), kind=kLoop, calls=%fused_computation.2 | loop fusion | flops 2358272 | bytes 1576960 | tf_op jit(solution)/shard_map/reduce_sum | solution.py:10
  2.5 34.0 %all_gather.6 = bf16[512,768]{1,0:T(8,128)(2,1)S(1)} all-gather(bf16[64,768]{1,0:T(8,128)(2,1)} %param.4), channel_id=1, replica_groups=mesh['blk'=8,'row'=4] {'blk'}, dimensions={0}, use_global_device_ids=true | all-gather | bytes 884736 | tf_op jit(solution)/shard_map/all_gather | solution.py:45
  36.4 0.1 constant_dynamic-update-slice_fusion.1
  36.5 0.0 copy-done.1
  36.5 0.0 copy-start
  36.5 32.2 %all_gather.7 = bf16[512,768]{1,0:T(8,128)(2,1)S(1)} all-gather(bf16[64,768]{1,0:T(8,128)(2,1)S(1)} %copy-done.1), channel_id=1, replica_groups=mesh['blk'=8,'row'=4] {'blk'}, dimensions={0}, use_global_device_ids=true | all-gather | bytes 884736 | tf_op jit(solution)/shard_map/all_gather | solution.py:46
  68.7 0.1 constant_dynamic-update-slice_fusion
  68.7 0.4 multiply_reduce_fusion
  69.1 0.0 copy-done
  69.1 1.8 %multiply_bitcast_fusion = f32[1024,1024]{0,1:T(8,128)S(1)} fusion(bf16[1024,768]{1,0:T(8,128)(2,1)S(1)} %constant_dynamic-update-slice_fusion, bf16[1024,768]{1,0:T(8,128)(2,1)S(1)} %copy-done, f32[1024]{0:T(1024)S(1)} %multiply_reduce_fusion, f32[1024]{0:T(1024)S(1)} %multiply_reduce_fusion.1), kind=kOutput, calls=%fused_computation | convolution fusion | flops 1614807040 | bytes 7348224 | tf_op jit(solution)/shard_map/dot_general | solution.py:17
  71.0 0.2 slice_reduce_fusion.1
  71.2 0.6 exponential_reduce_fusion.1
  71.8 5.8 %all-reduce.2 = (f32[1024]{0:T(1024)S(1)}, f32[1024]{0:T(1024)S(1)}) all-reduce(f32[1024]{0:T(1024)S(1)} %broadcast_maximum_fusion, f32[1024]{0:T(1024)S(1)} %broadcast_maximum_fusion.1), channel_id=1, replica_groups=mesh['blk'=8,'row'=4] {'row'}, use_global_device_ids=true, to_apply=%region_7.0 | all-reduce | flops 2048 | bytes 16384 | tf_op jit(solution)/shard_map/pmax | solution.py:50
  77.6 6.7 %all-reduce.1 = (f32[1024]{0:T(1024)S(1)}, f32[1024]{0:T(1024)S(1)}) all-reduce(f32[1024]{0:T(1024)S(1)} %get-tuple-element.15, f32[1024]{0:T(1024)S(1)} %get-tuple-element.16), channel_id=1, replica_groups=mesh['blk'=8,'row'=4] {'row'}, use_global_device_ids=true, to_apply=%region_9.0 | all-reduce | flops 2048 | bytes 16384 | tf_op jit(solution)/shard_map/psum | solution.py:51
  84.3 0.7 fusion
  85.0 0.0 copy-start.2
  85.0 22.0 %all-reduce = (f32[]{:T(128)}, f32[]{:T(128)}) all-reduce(f32[]{:T(128)} %get-tuple-element.7, f32[]{:T(128)} %get-tuple-element.6), channel_id=1, replica_groups=mesh['blk'=8,'row'=4] {'blk'}, use_global_device_ids=true, to_apply=%region_13.0 | all-reduce | flops 2 | bytes 16 | tf_op jit(solution)/shard_map/psum | solution.py:56
  109.5 0.6 subtract_divide_fusion
  110.2 0.0 copy-done.2
  (3 shorter events, 0.0 us)
Async XLA Ops:
  0.6 35.9 %copy-start.1 = (bf16[64,768]{1,0:T(8,128)(2,1)S(1)}, bf16[64,768]{1,0:T(8,128)(2,1)}, u32[]{:S(2)}) copy-start(bf16[64,768]{1,0:T(8,128)(2,1)} %param.5) | copy-start | bytes 294916
  36.5 32.6 %copy-start = (bf16[1024,768]{1,0:T(8,128)(2,1)S(1)}, bf16[1024,768]{1,0:T(8,128)(2,1)}, u32[]{:S(2)}) copy-start(bf16[1024,768]{1,0:T(8,128)(2,1)} %param.3) | copy-start | bytes 4718596
  85.0 25.2 %copy-start.2 = (f32[1024]{0:T(1024)}, f32[1024]{0:T(1024)S(1)}, u32[]{:S(2)}) copy-start(f32[1024]{0:T(1024)S(1)} %get-tuple-element.14) | copy-start | bytes 12292
where the time goes:
time: 110 us
  blocking collectives  101 us (92%)
  other arithmetic  4.29 us (4%)
  between operations  3.28 us (3%)
  matrix products  1.83 us (2%)
    all_gather x1, blocking collectives, body(): lax.all_gather(target_samples, 'blk', axis=0, tiled=True)  34 us
    all_gather x1, blocking collectives, body(): lax.all_gather(reference_samples, 'blk', axis=0, tiled=True)  32.2 us
    psum x1, blocking collectives, body(): lax.psum((jnp.sum(log_ratio), jnp.sum(jnp.square(log_ratio))), 'blk')  22 us
    psum x1, blocking collectives, body(): lax.psum((state[1] * jnp.exp(state[0] - high_target), state[3] * jnp.exp(...  6.7 us
    pmax x1, blocking collectives, body(): high_target, high_ref = lax.pmax((state[0], state[2]), 'row')  5.77 us

commit v1 on v0

v1 whole, which is shorter than its diff:
```python
import functools

import jax
import jax.numpy as jnp
from jax import lax
from jax.experimental import pallas as pl
from jax.experimental.pallas import tpu as pltpu
from jax.sharding import PartitionSpec as P

KERNEL_GAIN = 30.0
MESH = pl.DeviceIdType.MESH


def density_kernel(
    n_blk,
    n_row,
    pool_hbm,
    target_hbm,
    ref_hbm,
    ratio_out,
    std_out,
    pool,
    gathered,
    pool_norms,
    high,
    total,
    partials,
    stats,
    load_sem,
    right_send,
    left_send,
    line_recv,
    side_send,
    side_recv,
    row_send,
    row_recv,
    stat_send,
    stat_recv,
):
    me = lax.axis_index("blk")
    my_row = lax.axis_index("row")
    length = n_blk // 2
    place = me // 2
    side = lax.rem(me, 2)
    other = me + 1 - 2 * side
    rows, depth = pool.shape
    width = target_hbm.shape[0]
    factor = KERNEL_GAIN / depth
    sources = (target_hbm, ref_hbm)
    nt = (((1,), (1,)), ((), ()))

    pool_load = pltpu.make_async_copy(pool_hbm, pool, load_sem.at[2])
    pool_load.start()
    own_loads = [
        pltpu.make_async_copy(sources[k], gathered.at[place, k, side], load_sem.at[k]) for k in range(2)
    ]
    for load in own_loads:
        load.start()

    barrier = pltpu.get_barrier_semaphore()

    def greet(i, carry):
        pl.semaphore_signal(barrier, inc=1, device_id={"blk": lax.rem(me + i, n_blk)}, device_id_type=MESH)
        return carry

    lax.fori_loop(1, n_blk, greet, 0)
    for i in range(1, n_row):
        pl.semaphore_signal(barrier, inc=1, device_id={"row": lax.rem(my_row + i, n_row)}, device_id_type=MESH)
    pl.semaphore_wait(barrier, n_blk - 1 + n_row - 1)

    def line_copy(origin, k, src, step, sems):
        return pltpu.make_async_remote_copy(
            src_ref=src,
            dst_ref=gathered.at[origin, k, side],
            send_sem=sems.at[origin, k],
            recv_sem=line_recv.at[origin, k],
            device_id={"blk": me + 2 * step},
            device_id_type=MESH,
        )

    def side_copy(origin, k, src, to_side):
        return pltpu.make_async_remote_copy(
            src_ref=src,
            dst_ref=gathered.at[origin, k, to_side],
            send_sem=side_send.at[origin, k],
            recv_sem=side_recv.at[origin, k],
            device_id={"blk": other},
            device_id_type=MESH,
        )

    for k in range(2):

        @pl.when(place < length - 1)
        def _(k=k):
            line_copy(place, k, sources[k], 1, right_send).start()

        @pl.when(place > 0)
        def _(k=k):
            line_copy(place, k, sources[k], -1, left_send).start()

        side_copy(place, k, sources[k], side).start()

    pool_load.wait()
    ones = jnp.ones((8, depth), jnp.bfloat16)
    tile = 256 if rows % 256 == 0 else rows

    def norm_tile(i, carry):
        at = pl.multiple_of(i * tile, tile)
        squares = jnp.square(pool[pl.ds(at, tile), :].astype(jnp.float32))
        coarse = squares.astype(jnp.bfloat16)
        fine = (squares - coarse.astype(jnp.float32)).astype(jnp.bfloat16)
        sums = lax.dot_general(ones, coarse, nt, preferred_element_type=jnp.float32)
        sums = sums + lax.dot_general(ones, fine, nt, preferred_element_type=jnp.float32)
        pool_norms[:, pl.ds(at, tile)] = sums[0:1, :] * factor
        return carry

    lax.fori_loop(0, rows // tile, norm_tile, 0)
    high[...] = jnp.full_like(high, -1e30)
    total[...] = jnp.zeros_like(total)
    for load in own_loads:
        load.wait()

    def fold(origin):
        for k in range(2):
            side_copy(origin, k, gathered.at[origin, k, 1 - side], 1 - side).wait_recv()
        block = gathered[origin].reshape(4 * width, depth)
        norms = jnp.sum(jnp.square(block.astype(jnp.float32)), axis=1, keepdims=True)
        products = lax.dot_general(block, pool[...], nt, preferred_element_type=jnp.float32)
        scores_all = (2.0 * products - norms) * factor
        for k in range(2):
            scores = scores_all[2 * width * k : 2 * width * (k + 1), :]
            old = high[k : k + 1, :]
            new = jnp.maximum(old, jnp.max(scores, axis=0, keepdims=True))
            summed = jnp.sum(jnp.exp(scores - new), axis=0, keepdims=True)
            total[k : k + 1, :] = total[k : k + 1, :] * jnp.exp(old - new) + summed
            high[k : k + 1, :] = new

    def fold_step(step):
        @pl.when(place >= step)
        def _():
            fold(place - step)

        @pl.when((step > 0) & (place + step < length))
        def _():
            fold(place + step)

    def relay(step, carry):
        for k in range(2):

            @pl.when(place >= step)
            def _(k=k):
                origin = place - step
                block = gathered.at[origin, k, side]
                line_copy(origin, k, block, 1, right_send).wait_recv()

                @pl.when(place < length - 1)
                def _():
                    line_copy(origin, k, block, 1, right_send).start()

                side_copy(origin, k, block, side).start()

            @pl.when(place + step < length)
            def _(k=k):
                origin = place + step
                block = gathered.at[origin, k, side]
                line_copy(origin, k, block, -1, left_send).wait_recv()

                @pl.when(place > 0)
                def _():
                    line_copy(origin, k, block, -1, left_send).start()

                side_copy(origin, k, block, side).start()

        fold_step(step - 1)
        return carry

    lax.fori_loop(1, length, relay, 0)
    fold_step(length - 1)

    partials[my_row] = high[...] + jnp.log(total[...])

    def row_copy(slot, peer):
        return pltpu.make_async_remote_copy(
            src_ref=partials.at[slot],
            dst_ref=partials.at[slot],
            send_sem=row_send.at[peer],
            recv_sem=row_recv.at[slot],
            device_id={"row": peer},
            device_id_type=MESH,
        )

    peers = [lax.rem(my_row + i, n_row) for i in range(1, n_row)]
    for peer in peers:
        row_copy(my_row, peer).start()
    for peer in peers:
        row_copy(peer, peer).wait_recv()
    parts = [partials[i] for i in range(n_row)]
    top = functools.reduce(jnp.maximum, parts)
    mass = functools.reduce(jnp.add, [jnp.exp(part - top) for part in parts])
    logs = top + jnp.log(mass) - pool_norms[...]
    ratio = logs[0:1, :] - logs[1:2, :]
    ratio_out[...] = ratio

    local_mean = jnp.sum(ratio, axis=1, keepdims=True) / rows
    local_spread = jnp.sum(jnp.square(ratio - local_mean), axis=1, keepdims=True)
    lanes = stats.shape[2]
    stats[me, 0:1, :] = jnp.broadcast_to(local_mean, (1, lanes))
    stats[me, 1:2, :] = jnp.broadcast_to(local_spread, (1, lanes))

    def stat_copy(slot, peer):
        return pltpu.make_async_remote_copy(
            src_ref=stats.at[slot],
            dst_ref=stats.at[slot],
            send_sem=stat_send.at[peer],
            recv_sem=stat_recv.at[slot],
            device_id={"blk": peer},
            device_id_type=MESH,
        )

    def stat_start(i, carry):
        stat_copy(me, lax.rem(me + i, n_blk)).start()
        return carry

    def stat_wait(i, carry):
        peer = lax.rem(me + i, n_blk)
        stat_copy(peer, peer).wait_recv()
        return carry

    lax.fori_loop(1, n_blk, stat_start, 0)

    for k in range(2):

        def sent(origin, carry, k=k):
            @pl.when((origin <= place) & (place < length - 1))
            def _():
                line_copy(origin, k, gathered.at[origin, k, side], 1, right_send).wait_send()

            @pl.when((origin >= place) & (place > 0))
            def _():
                line_copy(origin, k, gathered.at[origin, k, side], -1, left_send).wait_send()

            side_copy(origin, k, gathered.at[origin, k, side], side).wait_send()
            return carry

        lax.fori_loop(0, length, sent, 0)
    for peer in peers:
        row_copy(my_row, peer).wait_send()

    lax.fori_loop(1, n_blk, stat_wait, 0)
    means = stats[:, 0, :]
    spreads = stats[:, 1, :]
    mean = jnp.sum(means, axis=0, keepdims=True) / n_blk
    spread = jnp.sum(spreads, axis=0, keepdims=True)
    spread = spread + rows * jnp.sum(jnp.square(means - mean), axis=0, keepdims=True)
    scale = jnp.sqrt(spread / (rows * n_blk) + 1e-05)
    std_out[...] = (ratio_out[...] - mean[:, 0:1]) / scale[:, 0:1]

    def stat_sent(i, carry):
        stat_copy(me, lax.rem(me + i, n_blk)).wait_send()
        return carry

    lax.fori_loop(1, n_blk, stat_sent, 0)


def body(n_blk, n_row, pool_embeds, target_samples, reference_samples):
    rows, depth = pool_embeds.shape
    width = target_samples.shape[0]
    length = n_blk // 2
    dma = pltpu.SemaphoreType.DMA
    flops = 2 * rows * depth * 2 * width * n_blk
    ratio, standardized = pl.pallas_call(
        functools.partial(density_kernel, n_blk, n_row),
        out_shape=[jax.ShapeDtypeStruct((1, rows), jnp.float32)] * 2,
        in_specs=[pl.BlockSpec(memory_space=pl.ANY)] * 3,
        out_specs=[pl.BlockSpec(memory_space=pltpu.VMEM)] * 2,
        scratch_shapes=[
            pltpu.VMEM((rows, depth), jnp.bfloat16),
            pltpu.VMEM((length, 2, 2, width, depth), jnp.bfloat16),
            pltpu.VMEM((1, rows), jnp.float32),
            pltpu.VMEM((2, rows), jnp.float32),
            pltpu.VMEM((2, rows), jnp.float32),
            pltpu.VMEM((n_row, 2, rows), jnp.float32),
            pltpu.VMEM((n_blk, 2, 128), jnp.float32),
            dma((3,)),
            dma((length, 2)),
            dma((length, 2)),
            dma((length, 2)),
            dma((length, 2)),
            dma((length, 2)),
            dma((n_row,)),
            dma((n_row,)),
            dma((n_blk,)),
            dma((n_blk,)),
        ],
        compiler_params=pltpu.CompilerParams(
            collective_id=0, has_side_effects=True, vmem_limit_bytes=62 * 1024 * 1024
        ),
        cost_estimate=pl.CostEstimate(flops=flops, bytes_accessed=2 * rows * depth, transcendentals=0),
    )(pool_embeds, target_samples, reference_samples)
    return ratio.reshape(rows), standardized.reshape(rows)


def solution(mesh):
    in_specs = (P("blk", None), P(("blk", "row"), None), P(("blk", "row"), None))
    out_specs = (P("blk"), P("blk"))
    part = functools.partial(body, mesh.shape["blk"], mesh.shape["row"])
    return jax.shard_map(part, mesh=mesh, in_specs=in_specs, out_specs=out_specs, check_vma=False)
```

time: 110 us -> 36.4 us (0.33)
  blocking collectives: 101 us -> 0 us
  Pallas kernels: 0 us -> 33 us
  other arithmetic: 4.29 us -> 0 us
  between operations: 3.28 us -> 0.64 us
  local copies, waits for them, and re-layouts: 0.12 us -> 2.53 us
  matrix products: 1.83 us -> 0 us
    all_gather x2 -> x0, blocking collectives: 66.1 us -> none  [the longest x1 34 us: body(): lax.all_gather(target_samples, 'blk', axis=0, tiled=True)]
    pallas_call x0 -> x1, Pallas kernels: none -> 33 us  [body(): pl.pallas_call(functools.partial(density_kernel, n_blk, n_row), out_shape...]
    psum x2 -> x0, blocking collectives: 28.7 us -> none  [the longest x1 22 us: body(): lax.psum((jnp.sum(log_ratio), jnp.sum(jnp.square(log_ratio))), 'blk')]
    pmax x1 -> x0, blocking collectives: 5.77 us -> none  [body(): high_target, high_ref = lax.pmax((state[0], state[2]), 'row')]
    reduce_sum x4 -> x0, other arithmetic: 3.45 us -> none  [the longest x1 1.82 us: make_fold(): pool_norms = jnp.sum(jnp.square(pool_rows.astype(jnp.float32)), axis=1)]
    unnamed x7 -> x2, local copies, waits for them, and re-layouts: 0.07 us -> 2.53 us
    dot_general x1 -> x0, matrix products: 1.83 us -> none  [fold(): products = jnp.dot(pool_rows, joined.T, preferred_element_type=jnp.float32)]
where the time goes in v1:
time: 36.4 us; the launch traced here: 36.1 us
  Pallas kernels  33 us (91%)
  local copies, waits for them, and re-layouts  2.53 us (7%)
  between operations  0.64 us (2%)
    pallas_call x1, Pallas kernels, body(): pl.pallas_call(functools.partial(density_kernel, n_blk, n_row), out_shape...  33 us
    unnamed x2, local copies, waits for them, and re-layouts  2.53 us

profile of v1, /device:TPU:0, one launch (start us, length us, event | category | flops | bytes accessed | tf_op | source)
XLA Modules:
  0.0 36.1 jit_solution(984164704487608348)
XLA Ops:
  0.6 33.0 %shard_map.50 = (f32[1,1024]{1,0:T(1,128)}, f32[1,1024]{1,0:T(1,128)}) custom-call(bf16[1024,768]{1,0:T(8,128)(2,1)} %pool_hbm.1, bf16[64,768]{1,0:T(8,128)(2,1)} %target_hbm.1, bf16[64,768]{1,0:T(8,128)(2,1)} %ref_hbm.1), custom_call_target="tpu_custom_call" | custom-call | flops 1610612736 | bytes 1572864 | tf_op jit(solution)/shard_map/pallas_call | solution.py:271
  33.6 1.3 %copy.7 = f32[1024]{0:T(1024)} copy(f32[1024]{0:T(1024)} %bitcast.3) | data formatting | bytes 8192
  34.9 1.3 %copy.8 = f32[1024]{0:T(1024)} copy(f32[1024]{0:T(1024)} %bitcast.2) | data formatting | bytes 8192
